TPU v7x, 128 devices: a whole 4x4x4 slice. The times are simulated.
128 devices in a mesh: replica: 16 (over y, z_hi, core), expert: 8 (over x, z_lo).
Axes of the slice: x: 4, y: 4, z: 4 (z_hi: 2, z_lo: 2; z = z_hi * 2 + z_lo), core: 2. Of those that a mesh axis runs over, the one named last changes fastest.
Arguments:
- tokens: bfloat16 [16384, 2048], P(('replica', 'expert')), may hold values from -6 to 6
- route_ids: int32 [16384, 1], P(('replica', 'expert')), may hold values from 0 to 7; in each aligned block of 128 rows (0 to 127, 128 to 255, ...) at most 24 rows name the same one
- route_logits: float32 [16384, 8], P(('replica', 'expert')), may hold values from -12 to 320, as said below
- grad_out: bfloat16 [16384, 2048], P(('replica', 'expert')), may hold values from -6 to 6
- w_gate: bfloat16 [16, 8, 2048, 768], P('replica', 'expert'), may hold values from -0.125 to 0.125
- w_up: bfloat16 [16, 8, 2048, 768], P('replica', 'expert'), may hold values from -0.125 to 0.125
- w_down: bfloat16 [16, 8, 768, 2048], P('replica', 'expert'), may hold values from -0.21875 to 0.21875
- drift: float32 [16, 2, 2048, 1024], P('replica', None, None, 'expert'), may hold values from -6 to 6
- outer: float32 [2, 2048, 1024], P(None, 'replica', 'expert'), may hold values from -6 to 6
- momentum: float32 [2, 2048, 1024], P(None, 'replica', 'expert'), may hold values from -4 to 4
- inner_now: bfloat16 [16, 2, 2048, 1024], P('replica', None, None, 'expert'), may hold values from -6 to 6
Outputs:
- grad_tokens: bfloat16 [16384, 2048], P(('replica', 'expert'))
- grad_logits: float32 [16384, 8], P(('replica', 'expert'))
- grad_gate: bfloat16 [16, 8, 2048, 768], P('replica', 'expert')
- grad_up: bfloat16 [16, 8, 2048, 768], P('replica', 'expert')
- grad_down: bfloat16 [16, 8, 768, 2048], P('replica', 'expert')
- new_outer: float32 [2, 2048, 1024], P(None, 'replica', 'expert')
- new_momentum: float32 [2, 2048, 1024], P(None, 'replica', 'expert')
- merged: bfloat16 [16, 2, 2048, 1024], P('replica', None, None, 'expert')
Inputs may be any that keep to these rules, and one draw needn't show every extreme that they name: `route_ids`: each token names one expert of its replica's group; the rows of one device name no expert more than 24 times, and in every draw the rows of some device name some expert exactly 24 times. `route_logits`: the first 1 column are the logits of the experts named in route_ids.
All inputs are finite; a program needn't handle non-finite values.
Results may differ from a plain program's by a relative error of at most 0.014.
Values may be sent and summed in bfloat16 or wider, within the bound.
A program may use at most 128 MiB of HBM per device.

v0:
```python
import jax
import jax.numpy as jnp
from jax import lax
from jax.sharding import PartitionSpec as P

D = 2048
FF = 768
TOP = 8
TOP_WIN = 1
EXP_DEV = 1


momentum_rate = 0.9
outer_rate = 0.7
mix_rate = 0.5


def slot_layout(route_ids, experts, capacity):
    flat_ids = route_ids.reshape(-1)
    onehot = (flat_ids[:, None] == jnp.arange(experts, dtype=jnp.int32)[None, :]).astype(jnp.int32)
    before = jnp.cumsum(onehot, axis=0) - onehot
    position = jnp.sum(before * onehot, axis=1)
    return flat_ids * capacity + position


def place_rows(pair_rows, slot_index, experts, capacity):
    buffer = jnp.zeros((experts * capacity, pair_rows.shape[1]), pair_rows.dtype)
    buffer = buffer.at[slot_index].set(pair_rows)
    return buffer.reshape(experts, capacity, pair_rows.shape[1])


def expert_front(received, w_gate, w_up, sources):
    item_count = received.shape[1]
    local_rows = received.reshape(sources, w_gate.shape[1], item_count, received.shape[2])
    gate_pre = jnp.einsum(
        "sexd,edf->sexf", local_rows, w_gate[0], preferred_element_type=jnp.float32
    )
    up_pre = jnp.einsum("sexd,edf->sexf", local_rows, w_up[0], preferred_element_type=jnp.float32)
    return (local_rows, gate_pre, up_pre)


def outer_step(drift, outer, momentum, inner_now):
    replicas = lax.axis_size("replica")
    drift_sum = lax.psum(drift[0].astype(jnp.bfloat16), "replica").astype(jnp.float32)
    states = (
        lax.all_gather(outer.astype(jnp.bfloat16), "replica", axis=1, tiled=True).astype(
            outer.dtype
        ),
        lax.all_gather(momentum.astype(jnp.bfloat16), "replica", axis=1, tiled=True).astype(
            momentum.dtype
        ),
    )
    average = drift_sum / replicas
    moment_whole = momentum_rate * states[1] + average
    new_whole = states[0] - outer_rate * (average + momentum_rate * moment_whole)
    row_count = outer.shape[1]
    first_row = lax.axis_index("replica") * row_count
    new_outer = lax.dynamic_slice_in_dim(new_whole, first_row, row_count, 1)
    new_moment = lax.dynamic_slice_in_dim(moment_whole, first_row, row_count, 1)
    merged = (mix_rate * inner_now.astype(jnp.float32) + (1.0 - mix_rate) * new_whole[None]).astype(
        jnp.bfloat16
    )
    return (new_outer, new_moment, merged)


def body(
    tokens,
    route_ids,
    route_logits,
    grad_out,
    w_gate,
    w_up,
    w_down,
    drift,
    outer,
    momentum,
    inner_now,
):
    token_count = tokens.shape[0]
    sources = lax.axis_size("expert")
    experts = EXP_DEV * sources
    capacity = 3 * token_count * TOP_WIN // (2 * experts)
    slot_index = slot_layout(route_ids, experts, capacity)
    pair_tokens = jnp.repeat(tokens, TOP_WIN, axis=0)
    pair_grads = jnp.repeat(grad_out, TOP_WIN, axis=0)
    send_rows = place_rows(pair_tokens, slot_index, experts, capacity)
    probability = jax.nn.softmax(route_logits, axis=-1)
    weighted = (probability[:, :TOP_WIN] * pair_grads.astype(jnp.float32)).astype(jnp.bfloat16)
    grad_send = place_rows(weighted, slot_index, experts, capacity)
    received = lax.all_to_all(send_rows, "expert", split_axis=0, concat_axis=0, tiled=True)
    item_count = received.shape[1]
    local_rows, gate_pre, up_pre = expert_front(received, w_gate, w_up, sources)
    active = (jax.nn.silu(gate_pre) * up_pre).astype(jnp.bfloat16)
    produced = jnp.einsum(
        "sexf,efd->sexd", active, w_down[0], preferred_element_type=jnp.float32
    ).astype(jnp.bfloat16)
    returned = lax.all_to_all(
        produced.reshape(received.shape), "expert", split_axis=0, concat_axis=0, tiled=True
    )
    returned, kept_rows, kept_gate, kept_up = (
        returned,
        received,
        gate_pre.reshape(experts, item_count, FF),
        up_pre.reshape(experts, item_count, FF),
    )
    grad_recv = lax.all_to_all(grad_send, "expert", split_axis=0, concat_axis=0, tiled=True)
    pair_out = returned.reshape(experts * capacity, D)[slot_index]
    prob_grad = jnp.sum(
        pair_grads.astype(jnp.float32) * pair_out.astype(jnp.float32), axis=1
    ).reshape(token_count, TOP_WIN)
    prob_full = jnp.concatenate(
        [prob_grad, jnp.zeros((token_count, TOP - TOP_WIN), jnp.float32)], axis=1
    )
    grad_logits = probability * (
        prob_full - jnp.sum(probability * prob_full, axis=1, keepdims=True)
    )
    resent = lax.all_to_all(send_rows, "expert", split_axis=0, concat_axis=0, tiled=True)
    local_rows, gate_pre, up_pre = expert_front(resent, w_gate, w_up, sources)
    sigmoid_gate = jax.nn.sigmoid(gate_pre)
    active = (jax.nn.silu(gate_pre) * up_pre).astype(jnp.bfloat16)
    upstream = grad_recv.reshape(sources, EXP_DEV, capacity, D)
    grad_active = jnp.einsum(
        "sexd,efd->sexf", upstream, w_down[0], preferred_element_type=jnp.float32
    )
    grad_down = jnp.einsum(
        "sexf,sexd->efd", active, upstream, preferred_element_type=jnp.float32
    ).astype(jnp.bfloat16)
    grad_gate_pre = (
        grad_active * up_pre * sigmoid_gate * (1.0 + gate_pre * (1.0 - sigmoid_gate))
    ).astype(jnp.bfloat16)
    grad_up_pre = (grad_active * jax.nn.silu(gate_pre)).astype(jnp.bfloat16)
    grad_gate = jnp.einsum(
        "sexd,sexf->edf", local_rows, grad_gate_pre, preferred_element_type=jnp.float32
    ).astype(jnp.bfloat16)
    grad_up = jnp.einsum(
        "sexd,sexf->edf", local_rows, grad_up_pre, preferred_element_type=jnp.float32
    ).astype(jnp.bfloat16)
    grad_inputs = (
        jnp.einsum("sexf,edf->sexd", grad_gate_pre, w_gate[0], preferred_element_type=jnp.float32)
        + jnp.einsum("sexf,edf->sexd", grad_up_pre, w_up[0], preferred_element_type=jnp.float32)
    ).astype(jnp.bfloat16)
    grad_back = lax.all_to_all(
        grad_inputs.reshape(experts, capacity, D), "expert", split_axis=0, concat_axis=0, tiled=True
    )
    pair_grad = grad_back.reshape(experts * capacity, D)[slot_index]
    grad_tokens = jnp.sum(
        pair_grad.reshape(token_count, TOP_WIN, D).astype(jnp.float32), axis=1
    ).astype(jnp.bfloat16)
    new_outer, new_moment, merged = outer_step(drift, outer, momentum, inner_now)
    return (
        grad_tokens,
        grad_logits,
        grad_gate[None],
        grad_up[None],
        grad_down[None],
        new_outer,
        new_moment,
        merged,
    )


def solution(mesh):
    in_specs = (
        P(("replica", "expert"), None),
        P(("replica", "expert"), None),
        P(("replica", "expert"), None),
        P(("replica", "expert"), None),
        P("replica", "expert", None, None),
        P("replica", "expert", None, None),
        P("replica", "expert", None, None),
        P("replica", None, None, "expert"),
        P(None, "replica", "expert"),
        P(None, "replica", "expert"),
        P("replica", None, None, "expert"),
    )
    out_specs = (
        P(("replica", "expert"), None),
        P(("replica", "expert"), None),
        P("replica", "expert", None, None),
        P("replica", "expert", None, None),
        P("replica", "expert", None, None),
        P(None, "replica", "expert"),
        P(None, "replica", "expert"),
        P("replica", None, None, "expert"),
    )
    return jax.shard_map(body, mesh=mesh, in_specs=in_specs, out_specs=out_specs, check_vma=False)
```

profile of v0, /device:TPU:1, one launch (start us, length us, event | category | flops | bytes accessed | tf_op | source)
XLA Modules:
  0.0 296.1 jit_solution(5049795512973729887)
XLA Ops:
  7.2 2.8 convert_bitcast_fusion
  10.6 2.8 scatter_custom_fusion.1
  13.4 6.2 %all-to-all-start.1 = ((bf16[8,24,2048]{2,1,0:T(8,128)(2,1)}), bf16[8,24,2048]{2,1,0:T(8,128)(2,1)}, u32[]{:S(2)}, u32[]{:S(2)}) async-start(bf16[8,24,2048]{2,1,0:T(8,128)(2,1)} %bitcast.117), calls=%async_computation.1 | async-start | bytes 1572864 | tf_op jit(solution)/shard_map/all_to_all | solution.py:117
  19.6 0.6 convert_element_type.96
  20.3 11.3 %all-to-all-done.1 = bf16[8,24,2048]{2,1,0:T(8,128)(2,1)} async-done(((bf16[8,24,2048]{2,1,0:T(8,128)(2,1)}), bf16[8,24,2048]{2,1,0:T(8,128)(2,1)}, u32[]{:S(2)}, u32[]{:S(2)}) %all-to-all-start.1) | async-done | bytes 786464 | tf_op jit(solution)/shard_map/all_to_all | solution.py:117
  31.6 3.1 %fusion.32 = f32[8,1,24,768]{3,2,0,1:T(8,128)S(1)} fusion(bf16[8,24,2048]{2,1,0:T(8,128)(2,1)} %all-to-all-done.1, bf16[1,1,2048,768]{3,2,1,0:T(8,128)(2,1)} %param.15), kind=kOutput, calls=%fused_computation.35 | convolution fusion | flops 603979776 | bytes 4521984 | tf_op jit(solution)/shard_map/sexd,edf->sexf/dot_general | solution.py:35
  34.8 2.2 fusion.26
  37.8 0.7 copy-done.8
  38.5 1.7 fusion.18
  40.2 4.2 %all-to-all-start.3 = ((bf16[8,24,2048]{2,1,0:T(8,128)(2,1)}), bf16[8,24,2048]{2,1,0:T(8,128)(2,1)}, u32[]{:S(2)}, u32[]{:S(2)}) async-start(bf16[8,24,2048]{2,1,0:T(8,128)(2,1)} %fusion.18), calls=%async_computation.3 | async-start | bytes 1572864 | tf_op jit(solution)/shard_map/all_to_all | solution.py:97
  44.5 0.6 convert_element_type.91
  45.2 10.5 %all-to-all-done.3 = bf16[8,24,2048]{2,1,0:T(8,128)(2,1)} async-done(((bf16[8,24,2048]{2,1,0:T(8,128)(2,1)}), bf16[8,24,2048]{2,1,0:T(8,128)(2,1)}, u32[]{:S(2)}, u32[]{:S(2)}) %all-to-all-start.3) | async-done | bytes 786464 | tf_op jit(solution)/shard_map/all_to_all | solution.py:97
  55.8 3.5 %gather_fusion.1 = bf16[128,2048]{1,0:T(8,128)(2,1)} fusion(bf16[192,2048]{1,0:T(8,128)(2,1)} %bitcast.33, s32[1024]{0:T(1024)S(1)} %pad_clamp_fusion), kind=kCustom, calls=%fused_computation.1 | custom fusion | bytes 1049088 | tf_op jit(solution)/shard_map/gather | solution.py:107
  59.2 1.4 fusion.36
  60.7 2.9 scatter_custom_fusion
  63.6 5.3 %all-to-all-start = ((bf16[8,24,2048]{2,1,0:T(8,128)(2,1)}), bf16[8,24,2048]{2,1,0:T(8,128)(2,1)}, u32[]{:S(2)}, u32[]{:S(2)}) async-start(bf16[8,24,2048]{2,1,0:T(8,128)(2,1)} %bitcast.116), calls=%async_computation | async-start | bytes 1572864 | tf_op jit(solution)/shard_map/all_to_all | solution.py:106
  69.5 91.3 %all-reduce.3.cloned.1.call-done = bf16[2,2048,128]{2,1,0:T(8,128)(2,1)} async-done(((bf16[2,2048,128]{2,1,0:T(8,128)(2,1)}), bf16[2,2048,128]{2,1,0:T(8,128)(2,1)}) %all-reduce.3.cloned.1.call-update) | async-done | bytes 1048592 | tf_op jit(solution)/shard_map/psum | solution.py:44
  160.8 49.9 %all-gather.5.cloned.1.call-done = bf16[2,2048,128]{2,1,0:T(8,128)(2,1)} async-done(((bf16[2,128,128]{2,1,0:T(8,128)(2,1)}), bf16[2,2048,128]{2,1,0:T(8,128)(2,1)}) %all-gather.5.cloned.1.call-update) | async-done | bytes 1048592 | tf_op jit(solution)/shard_map/all_gather | solution.py:49
  210.6 1.9 multiply_add_fusion
  212.5 0.7 constant_dynamic-slice_fusion.1
  213.2 44.5 %all-gather.3.cloned.1.call-done = bf16[2,2048,128]{2,1,0:T(8,128)(2,1)} async-done(((bf16[2,128,128]{2,1,0:T(8,128)(2,1)}), bf16[2,2048,128]{2,1,0:T(8,128)(2,1)}) %all-gather.3.cloned.1.call-update) | async-done | bytes 1048592 | tf_op jit(solution)/shard_map/all_gather | solution.py:46
  257.7 4.1 %fusion.25 = (bf16[1,2,2048,128]{3,2,1,0:T(8,128)(2,1)}, f32[2,2048,128]{2,1,0:T(8,128)S(1)}) fusion(bf16[1,2,2048,128]{3,2,1,0:T(8,128)(2,1)} %param.21, bf16[2,2048,128]{2,1,0:T(8,128)(2,1)} %all-gather.5.cloned.1.call-done, bf16[2,2048,128]{2,1,0:T(8,128)(2,1)} %all-reduce.3.cloned.1.call-done, bf16[2,2048,128]{2,1,0:T(8,128)(2,1)} %all-gather.3.cloned.1.call-done), kind=kLoop, calls=%fused_computation.27 | loop fusion | flops 7340032 | bytes 7340032 | tf_op jit(solution)/shard_map/convert_element_type | solution.py:60
  261.8 0.7 constant_dynamic-slice_fusion
  262.5 2.9 fusion.44
  265.4 1.2 fusion
  266.6 0.8 copy-done.3
  267.4 2.1 fusion.21
  269.5 4.4 %all-to-all-start.2 = ((bf16[8,24,2048]{2,1,0:T(8,128)(2,1)}), bf16[8,24,2048]{2,1,0:T(8,128)(2,1)}, u32[]{:S(2)}, u32[]{:S(2)}) async-start(bf16[8,24,2048]{2,1,0:T(8,128)(2,1)} %fusion.21), calls=%async_computation.2 | async-start | bytes 1572864 | tf_op jit(solution)/shard_map/all_to_all | solution.py:142
  273.9 4.0 %fusion.14 = bf16[1,1,768,2048]{3,2,1,0:T(8,128)(2,1)} fusion(bf16[8,24,768]{2,1,0:T(8,128)(2,1)} %copy-done.8, bf16[8,24,2048]{2,1,0:T(8,128)(2,1)} %all-to-all-done), kind=kOutput, calls=%fused_computation.21 | convolution fusion | flops 605552640 | bytes 4227072 | tf_op jit(solution)/shard_map/sexf,sexd->efd/dot_general | solution.py:125
  277.9 3.8 %fusion.13 = bf16[1,1,2048,768]{3,2,1,0:T(8,128)(2,1)} fusion(bf16[8,24,2048]{2,1,0:T(8,128)(2,1)} %all-to-all-done.1, bf16[8,24,768]{2,1,0:T(8,128)(2,1)S(1)} %copy-done.7), kind=kOutput, calls=%fused_computation.20 | convolution fusion | flops 605552640 | bytes 4227072 | tf_op jit(solution)/shard_map/sexd,sexf->edf/dot_general | solution.py:135
  281.7 3.8 %fusion.12 = bf16[1,1,2048,768]{3,2,1,0:T(8,128)(2,1)} fusion(bf16[8,24,2048]{2,1,0:T(8,128)(2,1)} %all-to-all-done.1, bf16[8,1,24,768]{3,2,0,1:T(8,128)(2,1)S(1)} %get-tuple-element.13), kind=kOutput, calls=%fused_computation.19 | convolution fusion | flops 605552640 | bytes 4227072 | tf_op jit(solution)/shard_map/sexd,sexf->edf/dot_general | solution.py:132
  286.1 3.5 %gather_fusion = bf16[128,2048]{1,0:T(8,128)(2,1)} fusion(bf16[192,2048]{1,0:T(8,128)(2,1)} %bitcast.28, s32[1024]{0:T(1024)S(1)} %pad_clamp_fusion), kind=kCustom, calls=%fused_computation | custom fusion | bytes 1049088 | tf_op jit(solution)/shard_map/gather | solution.py:145
  (43 shorter events, 2.7 us)
Async XLA Ops:
  7.2 31.3 %copy-start = (bf16[1,1,768,2048]{3,2,1,0:T(8,128)(2,1)S(1)}, bf16[1,1,768,2048]{3,2,1,0:T(8,128)(2,1)}, u32[]{:S(2)}) copy-start(bf16[1,1,768,2048]{3,2,1,0:T(8,128)(2,1)} %param.17) | copy-start | bytes 9437188
  7.2 2.9 copy-start.12
  7.2 153.6 %all-reduce.3.cloned.1.call-start = ((), (), s32[]{:S(2)}) async-start(), calls=%async_computation.5 | async-start | bytes 2097152 | tf_op jit(solution)/shard_map/psum | solution.py:44
  10.1 9.5 %copy-start.9 = (f32[2,128,128]{2,1,0:T(8,128)S(1)}, f32[2,128,128]{2,1,0:T(8,128)}, u32[]{:S(2)}) copy-start(f32[2,128,128]{2,1,0:T(8,128)} %param.20) | copy-start | bytes 393220
  13.4 18.2 %all-to-all-start.1 = ((bf16[8,24,2048]{2,1,0:T(8,128)(2,1)}), bf16[8,24,2048]{2,1,0:T(8,128)(2,1)}, u32[]{:S(2)}, u32[]{:S(2)}) async-start(bf16[8,24,2048]{2,1,0:T(8,128)(2,1)} %bitcast.117), calls=%async_computation.1 | async-start | bytes 1572864 | tf_op jit(solution)/shard_map/all_to_all | solution.py:117
  19.6 191.1 %all-gather.5.cloned.1.call-start = ((), (), s32[]{:S(2)}) async-start(), calls=%async_computation.6 | async-start | bytes 1114112 | tf_op jit(solution)/shard_map/all_gather | solution.py:49
  31.6 3.1 %copy-start.2 = (bf16[1,1,2048,768]{3,2,1,0:T(8,128)(2,1)S(1)}, bf16[1,1,2048,768]{3,2,1,0:T(8,128)(2,1)}, u32[]{:S(2)}) copy-start(bf16[1,1,2048,768]{3,2,1,0:T(8,128)(2,1)} %param.16) | copy-start | bytes 9437188
  34.8 2.2 copy-start.4
  37.0 0.8 copy-start.5
  37.8 0.7 copy-start.8
  38.5 6.0 %copy-start.10 = (f32[2,128,128]{2,1,0:T(8,128)S(1)}, f32[2,128,128]{2,1,0:T(8,128)}, u32[]{:S(2)}) copy-start(f32[2,128,128]{2,1,0:T(8,128)} %param.19) | copy-start | bytes 393220
  38.5 6.7 %copy-start.11 = (f32[128,8]{0,1:T(8,128)S(1)}, f32[128,8]{0,1:T(8,128)}, u32[]{:S(2)}) copy-start(f32[128,8]{0,1:T(8,128)} %param.13) | copy-start | bytes 12292
  40.2 15.6 %all-to-all-start.3 = ((bf16[8,24,2048]{2,1,0:T(8,128)(2,1)}), bf16[8,24,2048]{2,1,0:T(8,128)(2,1)}, u32[]{:S(2)}, u32[]{:S(2)}) async-start(bf16[8,24,2048]{2,1,0:T(8,128)(2,1)} %fusion.18), calls=%async_computation.3 | async-start | bytes 1572864 | tf_op jit(solution)/shard_map/all_to_all | solution.py:97
  44.4 213.3 %all-gather.3.cloned.1.call-start = ((), (), s32[]{:S(2)}) async-start(), calls=%async_computation.4 | async-start | bytes 1114112 | tf_op jit(solution)/shard_map/all_gather | solution.py:46
  63.6 198.9 %all-to-all-start = ((bf16[8,24,2048]{2,1,0:T(8,128)(2,1)}), bf16[8,24,2048]{2,1,0:T(8,128)(2,1)}, u32[]{:S(2)}, u32[]{:S(2)}) async-start(bf16[8,24,2048]{2,1,0:T(8,128)(2,1)} %bitcast.116), calls=%async_computation | async-start | bytes 1572864 | tf_op jit(solution)/shard_map/all_to_all | solution.py:106
  262.5 2.9 copy-start.1
  265.4 1.2 copy-start.6
  265.4 2.0 copy-start.3
  269.5 16.6 %all-to-all-start.2 = ((bf16[8,24,2048]{2,1,0:T(8,128)(2,1)}), bf16[8,24,2048]{2,1,0:T(8,128)(2,1)}, u32[]{:S(2)}, u32[]{:S(2)}) async-start(bf16[8,24,2048]{2,1,0:T(8,128)(2,1)} %fusion.21), calls=%async_computation.2 | async-start | bytes 1572864 | tf_op jit(solution)/shard_map/all_to_all | solution.py:142
  273.9 4.0 %copy-start.7 = (bf16[8,24,768]{2,1,0:T(8,128)(2,1)S(1)}, bf16[8,24,768]{2,1,0:T(8,128)(2,1)}, u32[]{:S(2)}) copy-start(bf16[8,24,768]{2,1,0:T(8,128)(2,1)} %copy-done.6) | copy-start | bytes 884740
Sparse Core Ops, SparseCore 0:
  11.1 149.6 all-reduce.2
  164.1 46.4 all-gather.4
  214.0 43.7 all-gather.2
where the time goes:
time: 297 us; the launch traced here: 296 us
  waiting for transfers between devices  208 us (70%)
  matrix products  24.7 us (8%)
  starting transfers between devices  20.2 us (7%)
  other arithmetic  15.7 us (5%)
  between operations  14 us (5%)
  local copies, waits for them, and re-layouts  13.3 us (4%)
    psum x1, waiting for transfers between devices, outer_step(): lax.psum(drift[0].astype(jnp.bfloat16), 'replica').astype(jnp.float32)  91.3 us
    all_gather x1, waiting for transfers between devices, outer_step(): lax.all_gather(momentum.astype(jnp.bfloat16), 'replica', axis=1, tiled=True)  49.9 us
    all_gather x1, waiting for transfers between devices, outer_step(): lax.all_gather(outer.astype(jnp.bfloat16), 'replica', axis=1, tiled=True)  44.5 us
    all_to_all x1, waiting for transfers between devices, body(): lax.all_to_all(send_rows, 'expert', split_axis=0, concat_axis=0, tiled=True)  11.3 us
    all_to_all x1, waiting for transfers between devices, body(): lax.all_to_all(produced.reshape(received.shape), 'expert', split_axis=0,...  10.5 us
    all_to_all x1, starting transfers between devices, body(): lax.all_to_all(send_rows, 'expert', split_axis=0, concat_axis=0, tiled=True)  6.2 us
  transfers between devices with their start and end apart: 7, of which 6 were waited for; matrix products, arithmetic and copies ran while one was open for 13% of the time, Pallas kernels for 0%

commit v1 on v0

v1 whole, which is shorter than its diff:
```python
import jax
import jax.numpy as jnp
from jax import lax
from jax.experimental import pallas as pl
from jax.experimental.pallas import tpu as pltpu
from jax.sharding import PartitionSpec as P

MESH = pl.DeviceIdType.MESH
D = 2048
FF = 768
HALF = D // 2
CAP = 24
BLOCKS = 8
ROWS = BLOCKS * CAP
GROUP = 4
GROUP_ROWS = GROUP * CAP
REPLICAS = 16

momentum_rate = 0.9
outer_rate = 0.7
mix_rate = 0.5

OFFSETS = ((1, 0), (3, 0), (1, 1), (3, 1), (2, 0), (2, 1), (0, 1), (0, 0))
OWN = 7


def f32(value):
    return value.astype(jnp.float32)


def to_wire(rows):
    blocks = rows.reshape(-1, CAP, D)
    return jnp.concatenate([blocks[:, :, :HALF], blocks[:, :, HALF:]], axis=1).astype(jnp.bfloat16)


def from_wire(blocks):
    wide = f32(blocks)
    count = wide.shape[0]
    left = wide[:, :CAP, :].reshape(count * CAP, HALF)
    right = wide[:, CAP:, :].reshape(count * CAP, HALF)
    return jnp.concatenate([left, right], axis=1).astype(jnp.bfloat16)


def dot(left, right, left_axis=1, right_axis=0):
    return lax.dot_general(
        left, right, (((left_axis,), (right_axis,)), ((), ())), preferred_element_type=jnp.float32
    )


def exchange_kernel(
    ids_hbm, logits_hbm, tokens_hbm, grads_hbm, gate_hbm, up_hbm, down_hbm, drift_hbm, outer_hbm, momentum_hbm,
    x_out, weighted_out, active_out, dgate_out, dup_out, back_out, select_out, dots_out, average_out, whole_out,
    ids, logits, tokens, grads, gate_w, up_w, down_w, drift_mine, drift_other, outer, momentum,
    token_send, token_recv, weighted_send, weighted_recv, back_send, dots_send, dots_recv,
    core_send, core_recv, y_send, y_recv, z_send, z_recv,
    local_sem, send_sem, recv_sem, core_sems, y_sems, z_sems,
):
    replica = lax.axis_index("replica")
    expert = lax.axis_index("expert")
    my_y, my_zh, my_core = replica // 4, (replica // 2) % 2, replica % 2
    my_x, my_zl = expert // 2, expert % 2

    def peer(dx, dz):
        return (replica, ((my_x + dx) % 4) * 2 + (my_zl + dz) % 2)

    def twin(dy, dzh, dcore):
        return ((((my_y + dy) % 4) * 2 + (my_zh + dzh) % 2) * 2 + (my_core + dcore) % 2, expert)

    core_twin = twin(0, 0, 1)
    z_twin = twin(0, 1, 0)
    y_twins = [twin(dy, 0, 0) for dy in (1, 2, 3)]

    barrier = pltpu.get_barrier_semaphore()
    partners = [peer(*offset) for offset in OFFSETS[:OWN]] + y_twins + [core_twin, z_twin]
    for partner in partners:
        pl.semaphore_signal(barrier, inc=1, device_id=partner, device_id_type=MESH)

    loads = {}
    pairs = dict(
        ids=(ids_hbm, ids), tokens=(tokens_hbm, tokens), logits=(logits_hbm, logits), grads=(grads_hbm, grads),
        other0=(drift_hbm.at[0, :, 1 - my_core], drift_other.at[:, 0]),
        other1=(drift_hbm.at[1, :, 1 - my_core], drift_other.at[:, 1]),
        mine0=(drift_hbm.at[0, :, my_core], drift_mine.at[:, 0]),
        mine1=(drift_hbm.at[1, :, my_core], drift_mine.at[:, 1]),
        gate=(gate_hbm, gate_w), up=(up_hbm, up_w), down=(down_hbm, down_w),
        outer=(outer_hbm, outer), momentum=(momentum_hbm, momentum),
    )
    for number, (name, (source, target)) in enumerate(pairs.items()):
        loads[name] = pltpu.make_async_copy(source, target, local_sem.at[number])
        loads[name].start()

    def remote(source, target, sems, device):
        return pltpu.make_async_remote_copy(
            src_ref=source, dst_ref=target, send_sem=sems[0], recv_sem=sems[1], device_id=device, device_id_type=MESH
        )

    def spread(send, recv, kind, forward):
        copies = []
        for block, (dx, dz) in enumerate(OFFSETS[:OWN]):
            device = peer(dx, dz) if forward else peer(-dx % 4, -dz % 2)
            sems = (send_sem.at[kind, block], recv_sem.at[kind, block])
            copies.append(remote(send.at[block], recv.at[block], sems, device))
        return copies

    token_copies = spread(token_send, token_recv, 0, True)
    weighted_copies = spread(weighted_send, weighted_recv, 1, True)
    back_copies = spread(back_send, back_out, 2, False)
    dots_copies = spread(dots_send, dots_recv, 3, False)

    loads["ids"].wait()
    id_row = ids[...]
    row = lax.broadcasted_iota(jnp.int32, (16, 128), 0)
    named = jnp.full((16, 128), -1, jnp.int32)
    for block, offset in enumerate(OFFSETS):
        named = jnp.where(row == block, peer(*offset)[1], named)
    onehot = jnp.where(named == id_row, 1.0, 0.0)
    before_mask = lax.broadcasted_iota(jnp.int32, (128, 128), 0) < lax.broadcasted_iota(jnp.int32, (128, 128), 1)
    before = dot(onehot.astype(jnp.bfloat16), jnp.where(before_mask, 1.0, 0.0).astype(jnp.bfloat16))
    slot = jnp.sum(onehot * (before + f32(row) * CAP), axis=0, keepdims=True)
    slot_row = lax.broadcasted_iota(jnp.int32, (ROWS, 128), 0)
    select = jnp.where(slot_row == slot.astype(jnp.int32), 1.0, 0.0).astype(jnp.bfloat16)
    select_out[...] = select

    def place(part, values, send, recv):
        first = part * GROUP
        wire = to_wire(dot(select[first * CAP : (first + GROUP) * CAP], values))
        if part == 0:
            send[0:GROUP] = wire
        else:
            send[GROUP:OWN] = wire[: OWN - GROUP]
            recv[OWN] = wire[OWN - GROUP]

    loads["tokens"].wait()
    values = tokens[...]
    place(0, values, token_send, token_recv)
    pl.semaphore_wait(barrier, len(partners))
    for copy in token_copies[:GROUP]:
        copy.start()

    loads["logits"].wait()
    scores = logits[...]
    powers = jnp.exp(scores - jnp.max(scores, axis=0, keepdims=True))
    probability = powers / jnp.sum(powers, axis=0, keepdims=True)
    column = jnp.transpose(jnp.broadcast_to(probability[0:1, :], (128, 128)))
    loads["grads"].wait()
    weighted = (f32(grads[...]) * jnp.concatenate([column] * (D // 128), axis=1)).astype(jnp.bfloat16)
    place(0, weighted, weighted_send, weighted_recv)
    for copy in weighted_copies[:GROUP]:
        copy.start()
    place(1, values, token_send, token_recv)
    for copy in token_copies[GROUP:]:
        copy.start()
    place(1, weighted, weighted_send, weighted_recv)
    for copy in weighted_copies[GROUP:]:
        copy.start()

    core_sum = remote(core_send, core_recv, (core_sems.at[0], core_sems.at[1]), core_twin)
    loads["other0"].wait()
    loads["other1"].wait()
    core_send[...] = drift_other[...].astype(jnp.bfloat16)
    core_sum.start()
    loads["mine0"].wait()
    loads["mine1"].wait()
    core_sum.wait()
    y_send[...] = (drift_mine[...] + f32(core_recv[...])).astype(jnp.bfloat16)
    y_sum = []
    for step in range(3):
        there = (my_y + step + 1) % 4
        copy = remote(
            y_send.at[pl.ds(there * 2, 2)], y_recv.at[step], (y_sems.at[0, step], y_sems.at[1, step]), y_twins[step]
        )
        copy.start()
        y_sum.append(copy)

    def front(part):
        first = part * GROUP
        rows = pl.ds(first * CAP, GROUP_ROWS)
        if part == 0:
            for copy in token_copies[:GROUP]:
                copy.wait_recv()
        inputs = from_wire(token_recv[first : first + GROUP])
        x_out[rows, :] = inputs
        if part == 0:
            loads["gate"].wait()
            loads["up"].wait()
        gate = dot(inputs, gate_w[...])
        up = dot(inputs, up_w[...])
        sigmoid = 1.0 / (1.0 + jnp.exp(-gate))
        silu = gate * sigmoid
        active = silu * up
        active_out[rows, :] = active.astype(jnp.bfloat16)
        if part == 0:
            for copy in weighted_copies[:GROUP]:
                copy.wait_recv()
        upstream = from_wire(weighted_recv[first : first + GROUP])
        weighted_out[rows, :] = upstream
        if part == 0:
            loads["down"].wait()
        grad_active = dot(upstream, down_w[...], 1, 1)
        scalars = jnp.sum(grad_active * active, axis=1, keepdims=True)
        dgate = (grad_active * up * sigmoid * (1.0 + gate * (1.0 - sigmoid))).astype(jnp.bfloat16)
        dup = (grad_active * silu).astype(jnp.bfloat16)
        dgate_out[rows, :] = dgate
        dup_out[rows, :] = dup
        lane = lax.broadcasted_iota(jnp.int32, (8, 128), 1)
        for block in range(GROUP):
            eights = [jnp.broadcast_to(scalars[block * CAP + 8 * i : block * CAP + 8 * i + 8], (8, 128)) for i in range(3)]
            packed = jnp.where(lane < 32, eights[0], jnp.where(lane < 64, eights[1], eights[2]))
            if first + block == OWN:
                dots_recv[OWN] = packed
            else:
                dots_send[first + block] = packed
        wire = to_wire(dot(dgate, gate_w[...], 1, 1) + dot(dup, up_w[...], 1, 1))
        if part == 0:
            back_send[0:GROUP] = wire
        else:
            back_send[GROUP:OWN] = wire[: OWN - GROUP]
            back_out[OWN] = wire[OWN - GROUP]

    front(0)
    for copy in token_copies[GROUP:] + weighted_copies[GROUP:]:
        copy.wait_recv()
    for copy in back_copies[:GROUP] + dots_copies[:GROUP]:
        copy.start()

    for copy in y_sum:
        copy.wait()
    mine = pl.ds(my_y * 2, 2)
    y_total = drift_mine[mine] + f32(core_recv[mine])
    for step in range(3):
        y_total += f32(y_recv[step])
    z_send[...] = y_total.astype(jnp.bfloat16)
    z_sum = remote(z_send.at[1 - my_zh], z_recv, (z_sems.at[0], z_sems.at[1]), z_twin)
    z_sum.start()
    near = jnp.where(my_zh == 0, y_total[0], y_total[1])
    z_sum.wait()
    average = (near + f32(z_recv[...])) / REPLICAS
    average_out[...] = average
    loads["outer"].wait()
    loads["momentum"].wait()
    moment = momentum_rate * momentum[...] + average
    stepped = outer[...] - outer_rate * (average + momentum_rate * moment)
    whole_out[my_core, my_y, my_zh] = stepped.astype(jnp.bfloat16)
    piece = whole_out.at[my_core, my_y, my_zh]
    z_gather = remote(piece, piece, (z_sems.at[2], z_sems.at[3]), z_twin)
    z_gather.start()

    front(1)
    for copy in back_copies[GROUP:] + dots_copies[GROUP:]:
        copy.start()

    z_gather.wait()
    y_gather = []
    for step in range(3):
        piece = whole_out.at[my_core, my_y]
        copy = remote(piece, piece, (y_sems.at[2, step], y_sems.at[3, step]), y_twins[step])
        copy.start()
        y_gather.append(copy)
    for copy in y_gather:
        copy.wait()
    piece = whole_out.at[my_core]
    core_gather = remote(piece, piece, (core_sems.at[2], core_sems.at[3]), core_twin)
    core_gather.start()

    for copy in token_copies + weighted_copies:
        copy.wait_send()
    for copy in dots_copies:
        copy.wait()
    for block in range(BLOCKS):
        for i in range(3):
            start = block * CAP + 8 * i
            dots_out[start : start + 8, :] = jnp.broadcast_to(dots_recv[block][:, 32 * i : 32 * i + 1], (8, 128))
    for copy in back_copies:
        copy.wait()
    core_gather.wait()


def exchange(ids, logits, tokens, grads, w_gate, w_up, w_down, drift, outer, momentum):
    bf16, wide = jnp.bfloat16, jnp.float32
    anywhere = pl.BlockSpec(memory_space=pl.ANY)
    inside = pl.BlockSpec(memory_space=pltpu.VMEM)
    outs = [
        ((ROWS, D), bf16), ((ROWS, D), bf16), ((ROWS, FF), bf16), ((ROWS, FF), bf16), ((ROWS, FF), bf16),
        ((BLOCKS, 2 * CAP, HALF), bf16), ((ROWS, 128), bf16), ((ROWS, 128), wide),
        ((2, 128, 128), wide), ((2, 4, 2, 2, 128, 128), bf16),
    ]
    wire = pltpu.VMEM((BLOCKS, 2 * CAP, HALF), bf16)
    dots = pltpu.VMEM((BLOCKS, 8, 128), wide)
    dma = pltpu.SemaphoreType.DMA
    return pl.pallas_call(
        exchange_kernel,
        out_shape=[jax.ShapeDtypeStruct(*out) for out in outs],
        in_specs=[anywhere] * 10,
        out_specs=[inside] * len(outs),
        scratch_shapes=[
            pltpu.VMEM((1, 128), jnp.int32), pltpu.VMEM((8, 128), wide),
            pltpu.VMEM((128, D), bf16), pltpu.VMEM((128, D), bf16),
            pltpu.VMEM((D, FF), bf16), pltpu.VMEM((D, FF), bf16), pltpu.VMEM((FF, D), bf16),
            pltpu.VMEM((8, 2, 128, 128), wide), pltpu.VMEM((8, 2, 128, 128), wide),
            pltpu.VMEM((2, 128, 128), wide), pltpu.VMEM((2, 128, 128), wide),
            wire, wire, wire, wire, wire, dots, dots,
            pltpu.VMEM((8, 2, 128, 128), bf16), pltpu.VMEM((8, 2, 128, 128), bf16),
            pltpu.VMEM((8, 2, 128, 128), bf16), pltpu.VMEM((3, 2, 2, 128, 128), bf16),
            pltpu.VMEM((2, 2, 128, 128), bf16), pltpu.VMEM((2, 128, 128), bf16),
            dma((13,)), dma((4, OWN)), dma((4, OWN)), dma((4,)), dma((4, 3)), dma((4,)),
        ],
        compiler_params=pltpu.CompilerParams(
            collective_id=0, has_side_effects=True, vmem_limit_bytes=44 << 20
        ),
        cost_estimate=pl.CostEstimate(flops=5 * 2 * ROWS * D * FF, bytes_accessed=16 << 20, transcendentals=ROWS * FF),
    )(ids, logits, tokens, grads, w_gate, w_up, w_down, drift, outer, momentum)


STEPS = 4


def finish_kernel(
    x, weighted, active, dgate, dup, back, select, dots, average, whole, logits, outer, momentum, inner,
    grad_tokens, grad_logits, grad_gate, grad_up, grad_down, new_outer, new_momentum, merged,
):
    step = pl.program_id(0)
    grad_gate[...] = dot(x[...], dgate[...], 0, 0).astype(jnp.bfloat16)
    grad_up[...] = dot(x[...], dup[...], 0, 0).astype(jnp.bfloat16)
    grad_down[...] = dot(active[...], weighted[...], 0, 0).astype(jnp.bfloat16)
    for layer in range(2):
        for zh in range(2):
            for core in range(2):
                rows = pl.ds((zh * 2 + core) * 128, 128)
                merged[layer, rows, :] = (
                    mix_rate * f32(inner[layer, rows, :]) + (1.0 - mix_rate) * f32(whole[core, 0, zh, layer])
                ).astype(jnp.bfloat16)

    @pl.when(step == 0)
    def _():
        grad_tokens[...] = dot(select[...], from_wire(back[...]), 0, 0).astype(jnp.bfloat16)
        scores = logits[...]
        powers = jnp.exp(scores - jnp.max(scores, axis=0, keepdims=True))
        probability = powers / jnp.sum(powers, axis=0, keepdims=True)
        scalar = jnp.sum(f32(select[...]) * dots[...], axis=0, keepdims=True)
        first = lax.broadcasted_iota(jnp.int32, (8, 128), 0) == 0
        grad_logits[...] = jnp.where(first, scalar * (1.0 - probability), -probability * scalar)
        moment = momentum_rate * momentum[...] + average[...]
        new_momentum[...] = moment
        new_outer[...] = outer[...] - outer_rate * (average[...] + momentum_rate * moment)


def finish(x, weighted, active, dgate, dup, back, select, dots, average, whole, logits, outer, momentum, inner):
    bf16, wide = jnp.bfloat16, jnp.float32

    def fixed(shape):
        return pl.BlockSpec(shape, lambda i: (0,) * len(shape))

    x_cols, rows = D // STEPS, D // STEPS
    return pl.pallas_call(
        finish_kernel,
        grid=(STEPS,),
        out_shape=[
            jax.ShapeDtypeStruct((128, D), bf16), jax.ShapeDtypeStruct((8, 128), wide),
            jax.ShapeDtypeStruct((D, FF), bf16), jax.ShapeDtypeStruct((D, FF), bf16),
            jax.ShapeDtypeStruct((FF, D), bf16), jax.ShapeDtypeStruct((2, 128, 128), wide),
            jax.ShapeDtypeStruct((2, 128, 128), wide), jax.ShapeDtypeStruct((2, D, 128), bf16),
        ],
        in_specs=[
            pl.BlockSpec((ROWS, x_cols), lambda i: (0, i)), pl.BlockSpec((ROWS, x_cols), lambda i: (0, i)),
            fixed((ROWS, FF)), fixed((ROWS, FF)), fixed((ROWS, FF)),
            fixed((BLOCKS, 2 * CAP, HALF)), fixed((ROWS, 128)), fixed((ROWS, 128)), fixed((2, 128, 128)),
            pl.BlockSpec((2, 1, 2, 2, 128, 128), lambda i: (0, i, 0, 0, 0, 0)),
            fixed((8, 128)), fixed((2, 128, 128)), fixed((2, 128, 128)),
            pl.BlockSpec((2, rows, 128), lambda i: (0, i, 0)),
        ],
        out_specs=[
            fixed((128, D)), fixed((8, 128)),
            pl.BlockSpec((x_cols, FF), lambda i: (i, 0)), pl.BlockSpec((x_cols, FF), lambda i: (i, 0)),
            pl.BlockSpec((FF, x_cols), lambda i: (0, i)), fixed((2, 128, 128)), fixed((2, 128, 128)),
            pl.BlockSpec((2, rows, 128), lambda i: (0, i, 0)),
        ],
        compiler_params=pltpu.CompilerParams(vmem_limit_bytes=44 << 20),
        cost_estimate=pl.CostEstimate(flops=3 * 2 * ROWS * D * FF, bytes_accessed=18 << 20, transcendentals=1024),
    )(x, weighted, active, dgate, dup, back, select, dots, average, whole, logits, outer, momentum, inner)


def body(tokens, route_ids, route_logits, grad_out, w_gate, w_up, w_down, drift, outer, momentum, inner_now):
    logits = route_logits.T
    sent = exchange(
        route_ids.reshape(1, 128), logits, tokens, grad_out, w_gate[0, 0], w_up[0, 0], w_down[0, 0],
        drift.reshape(2, 8, 2, 128, 128), outer, momentum,
    )
    grad_tokens, grad_logits, grad_gate, grad_up, grad_down, new_outer, new_momentum, merged = finish(
        *sent, logits, outer, momentum, inner_now[0]
    )
    return (
        grad_tokens, grad_logits.T, grad_gate[None, None], grad_up[None, None], grad_down[None, None],
        new_outer, new_momentum, merged[None],
    )


def solution(mesh):
    both = P(("replica", "expert"), None)
    pair = P("replica", "expert", None, None)
    part = P("replica", None, None, "expert")
    shard = P(None, "replica", "expert")
    in_specs = (both, both, both, both, pair, pair, pair, part, shard, shard, part)
    out_specs = (both, both, pair, pair, pair, shard, shard, part)
    return jax.shard_map(body, mesh=mesh, in_specs=in_specs, out_specs=out_specs, check_vma=False)
```

time: 297 us -> 62.8 us (0.21)
  waiting for transfers between devices: 208 us -> 0 us
  Pallas kernels: 0 us -> 55 us
  matrix products: 24.7 us -> 0 us
  starting transfers between devices: 20.2 us -> 0 us
  other arithmetic: 15.7 us -> 0 us
  between operations: 14 us -> 0.69 us
  local copies, waits for them, and re-layouts: 13.3 us -> 6.83 us
    all_gather x2 -> x0, waiting for transfers between devices: 94.4 us -> none  [the longest x1 49.9 us: outer_step(): lax.all_gather(momentum.astype(jnp.bfloat16), 'replica', axis=1, tiled=True)]
    psum x1 -> x0, waiting for transfers between devices: 91.3 us -> none  [outer_step(): lax.psum(drift[0].astype(jnp.bfloat16), 'replica').astype(jnp.float32)]
    pallas_call x0 -> x2, Pallas kernels: none -> 55 us  [the longest x1 48.7 us: exchange(): pl.pallas_call(exchange_kernel, out_shape=[jax.ShapeDtypeStruct(*out) for...]
    dot_general x9 -> x0, matrix products: 24.7 us -> none  [the longest x1 3.95 us: body(): jnp.einsum('sexf,sexd->efd', active, upstream, preferred_element_type=jnp...]
    all_to_all x4 -> x0, waiting for transfers between devices: 22.4 us -> none  [the longest x1 11.3 us: body(): lax.all_to_all(send_rows, 'expert', split_axis=0, concat_axis=0, tiled=True)]
    all_to_all x4 -> x0, starting transfers between devices: 20.1 us -> none  [the longest x1 6.2 us: body(): lax.all_to_all(send_rows, 'expert', split_axis=0, concat_axis=0, tiled=True)]
    convert_element_type x5 -> x0, other arithmetic: 8.3 us -> none  [the longest x1 4.09 us: outer_step(): (mix_rate * inner_now.astype(jnp.float32) + (1.0 - mix_rate) * new_whole[...]
    gather x2 -> x0, local copies, waits for them, and re-layouts: 6.93 us -> none  [the longest x1 3.47 us: body(): pair_out = returned.reshape(experts * capacity, D)[slot_index]]
  transfers between devices with their start and end apart: 7 -> 0, of which waited for: 6 -> 0; matrix products, arithmetic and copies ran while one was open for 13% -> 0% of each run, Pallas kernels for 0% -> 0%
where the time goes in v1:
time: 62.8 us; the launch traced here: 62.5 us
  Pallas kernels  55 us (88%)
  local copies, waits for them, and re-layouts  6.83 us (11%)
  between operations  0.69 us (1%)
    pallas_call x1, Pallas kernels, exchange(): pl.pallas_call(exchange_kernel, out_shape=[jax.ShapeDtypeStruct(*out) for...  48.7 us
    unnamed x20, local copies, waits for them, and re-layouts  6.83 us
    pallas_call x1, Pallas kernels, finish(): pl.pallas_call(finish_kernel, grid=(STEPS,), out_shape=[jax.ShapeDtypeStr...  6.34 us

profile of v1, /device:TPU:1, one launch (start us, length us, event | category | flops | bytes accessed | tf_op | source)
XLA Modules:
  0.0 62.5 jit_solution(5770169767714333367)
XLA Ops:
  0.6 0.0 copy-start
  0.6 1.6 %copy-done = f32[1,2,2048,128]{3,2,1,0:T(8,128)S(1)} copy-done((f32[1,2,2048,128]{3,2,1,0:T(8,128)S(1)}, f32[1,2,2048,128]{3,2,1,0:T(8,128)}, u32[]{:S(2)}) %copy-start) | copy-done | bytes 2097176
  2.2 0.0 copy-start.1
  2.2 1.0 %copy-done.1 = bf16[128,2048]{1,0:T(8,128)(2,1)S(1)} copy-done((bf16[128,2048]{1,0:T(8,128)(2,1)S(1)}, bf16[128,2048]{1,0:T(8,128)(2,1)}, u32[]{:S(2)}) %copy-start.1) | copy-done | bytes 524312
  3.3 0.0 copy-start.2
  3.3 1.0 %copy-done.2 = bf16[128,2048]{1,0:T(8,128)(2,1)S(1)} copy-done((bf16[128,2048]{1,0:T(8,128)(2,1)S(1)}, bf16[128,2048]{1,0:T(8,128)(2,1)}, u32[]{:S(2)}) %copy-start.2) | copy-done | bytes 524312
  4.3 0.0 copy-start.3
  4.3 0.9 %copy-done.3 = f32[2,128,128]{2,1,0:T(8,128)S(1)} copy-done((f32[2,128,128]{2,1,0:T(8,128)S(1)}, f32[2,128,128]{2,1,0:T(8,128)}, u32[]{:S(2)}) %copy-start.3) | copy-done | bytes 131096
  5.2 0.0 copy-start.5
  5.2 0.9 %copy-done.5 = f32[2,128,128]{2,1,0:T(8,128)S(1)} copy-done((f32[2,128,128]{2,1,0:T(8,128)S(1)}, f32[2,128,128]{2,1,0:T(8,128)}, u32[]{:S(2)}) %copy-start.5) | copy-done | bytes 131096
  6.1 0.0 copy-start.7
  6.1 0.7 %copy-done.7 = f32[128,8]{0,1:T(8,128)S(1)} copy-done((f32[128,8]{0,1:T(8,128)S(1)}, f32[128,8]{0,1:T(8,128)}, u32[]{:S(2)}) %copy-start.7) | copy-done | bytes 4120
  6.8 0.0 copy-start.8
  6.8 0.7 %copy-done.8 = s32[128,1]{0,1:T(1,128)S(1)} copy-done((s32[128,1]{0,1:T(1,128)S(1)}, s32[128,1]{0,1:T(1,128)}, u32[]{:S(2)}) %copy-start.8) | copy-done | bytes 536
  7.5 0.0 copy-start.4
  7.5 0.0 copy-start.6
  7.5 0.0 copy-start.9
  7.5 48.7 %shard_map.170 = (bf16[192,2048]{1,0:T(8,128)(2,1)S(1)}, bf16[192,2048]{1,0:T(8,128)(2,1)S(1)}, bf16[192,768]{1,0:T(8,128)(2,1)S(1)}, bf16[192,768]{1,0:T(8,128)...) custom-call(s32[1,128]{1,0:T(1,128)S(1)} %bitcast.15, ...), custom_call_target="tpu_custom_call" | custom-call | flops 3019898880 | bytes 16777216 | tf_op jit(solution)/shard_map/pallas_call | solution.py:290
  56.2 0.0 copy-done.4
  56.2 0.0 copy-done.6
  56.2 0.0 copy-done.9
  56.2 6.3 %shard_map.171 = (bf16[128,2048]{1,0:T(8,128)(2,1)}, f32[8,128]{1,0:T(8,128)}, bf16[2048,768]{1,0:T(8,128)(2,1)}, bf16[2048,768]{1,0:T(8,128)(2,1)}, bf16[768,20...) custom-call(bf16[192,2048]{1,0:T(8,128)(2,1)S(1)} %get-tuple-element.26.x, ...), custom_call_target="tpu_custom_call" | custom-call | flops 1811939328 | bytes 18874368 | tf_op jit(solution)/shard_map/pallas_call | solution.py:354
Async XLA Ops:
  0.6 1.6 %copy-start = (f32[1,2,2048,128]{3,2,1,0:T(8,128)S(1)}, f32[1,2,2048,128]{3,2,1,0:T(8,128)}, u32[]{:S(2)}) copy-start(f32[1,2,2048,128]{3,2,1,0:T(8,128)} %param.18) | copy-start | bytes 6291460
  2.2 1.0 %copy-start.1 = (bf16[128,2048]{1,0:T(8,128)(2,1)S(1)}, bf16[128,2048]{1,0:T(8,128)(2,1)}, u32[]{:S(2)}) copy-start(bf16[128,2048]{1,0:T(8,128)(2,1)} %tokens_hbm.1) | copy-start | bytes 1572868
  3.3 1.0 %copy-start.2 = (bf16[128,2048]{1,0:T(8,128)(2,1)S(1)}, bf16[128,2048]{1,0:T(8,128)(2,1)}, u32[]{:S(2)}) copy-start(bf16[128,2048]{1,0:T(8,128)(2,1)} %grads_hbm.1) | copy-start | bytes 1572868
  4.3 0.9 %copy-start.3 = (f32[2,128,128]{2,1,0:T(8,128)S(1)}, f32[2,128,128]{2,1,0:T(8,128)}, u32[]{:S(2)}) copy-start(f32[2,128,128]{2,1,0:T(8,128)} %outer.1) | copy-start | bytes 393220
  5.2 0.9 %copy-start.5 = (f32[2,128,128]{2,1,0:T(8,128)S(1)}, f32[2,128,128]{2,1,0:T(8,128)}, u32[]{:S(2)}) copy-start(f32[2,128,128]{2,1,0:T(8,128)} %momentum.1) | copy-start | bytes 393220
  6.1 0.7 %copy-start.7 = (f32[128,8]{0,1:T(8,128)S(1)}, f32[128,8]{0,1:T(8,128)}, u32[]{:S(2)}) copy-start(f32[128,8]{0,1:T(8,128)} %param.13) | copy-start | bytes 12292
  6.8 0.7 %copy-start.8 = (s32[128,1]{0,1:T(1,128)S(1)}, s32[128,1]{0,1:T(1,128)}, u32[]{:S(2)}) copy-start(s32[128,1]{0,1:T(1,128)} %param.12) | copy-start | bytes 1540
  7.5 48.7 %copy-start.4 = (f32[2,128,128]{2,1,0:T(8,128)S(1)}, f32[2,128,128]{2,1,0:T(8,128)}, u32[]{:S(2)}) copy-start(f32[2,128,128]{2,1,0:T(8,128)} %outer.1) | copy-start | bytes 393220
  7.5 48.7 %copy-start.6 = (f32[2,128,128]{2,1,0:T(8,128)S(1)}, f32[2,128,128]{2,1,0:T(8,128)}, u32[]{:S(2)}) copy-start(f32[2,128,128]{2,1,0:T(8,128)} %momentum.1) | copy-start | bytes 393220
  7.5 48.7 %copy-start.9 = (bf16[1,2,2048,128]{3,2,1,0:T(8,128)(2,1)S(1)}, bf16[1,2,2048,128]{3,2,1,0:T(8,128)(2,1)}, u32[]{:S(2)}) copy-start(bf16[1,2,2048,128]{3,2,1,0:T(8,128)(2,1)} %param.21) | copy-start | bytes 3145732

commit v2 on v1

--- a/solution.py
+++ b/solution.py
@@ -49,8 +49,8 @@
 
 def exchange_kernel(
     ids_hbm, logits_hbm, tokens_hbm, grads_hbm, gate_hbm, up_hbm, down_hbm, drift_hbm, outer_hbm, momentum_hbm,
-    x_out, weighted_out, active_out, dgate_out, dup_out, back_out, select_out, dots_out, average_out, whole_out,
-    ids, logits, tokens, grads, gate_w, up_w, down_w, drift_mine, drift_other, outer, momentum,
+    grad_gate_out, grad_up_out, grad_down_out, back_out, select_out, dots_out, average_out, whole_out,
+    x_keep, weighted_keep, active_keep, dgate_keep, dup_keep, y_total, ids, logits, tokens, grads, gate_w, up_w, down_w, drift_mine, drift_other, outer, momentum,
     token_send, token_recv, weighted_send, weighted_recv, back_send, dots_send, dots_recv,
     core_send, core_recv, y_send, y_recv, z_send, z_recv,
     local_sem, send_sem, recv_sem, core_sems, y_sems, z_sems,
@@ -136,6 +136,12 @@
     pl.semaphore_wait(barrier, len(partners))
     for copy in token_copies[:GROUP]:
         copy.start()
+
+    core_sum = remote(core_send, core_recv, (core_sems.at[0], core_sems.at[1]), core_twin)
+    loads["other0"].wait()
+    loads["other1"].wait()
+    core_send[...] = drift_other[...].astype(jnp.bfloat16)
+    core_sum.start()
 
     loads["logits"].wait()
     scores = logits[...]
@@ -151,14 +157,9 @@
     for copy in token_copies[GROUP:]:
         copy.start()
     place(1, weighted, weighted_send, weighted_recv)
-    for copy in weighted_copies[GROUP:]:
-        copy.start()
-
-    core_sum = remote(core_send, core_recv, (core_sems.at[0], core_sems.at[1]), core_twin)
-    loads["other0"].wait()
-    loads["other1"].wait()
-    core_send[...] = drift_other[...].astype(jnp.bfloat16)
-    core_sum.start()
+    weighted_copies[GROUP].start()
+    weighted_copies[GROUP + 1].start()
+
     loads["mine0"].wait()
     loads["mine1"].wait()
     core_sum.wait()
@@ -172,14 +173,14 @@
         copy.start()
         y_sum.append(copy)
 
-    def front(part):
+    def front_in(part):
         first = part * GROUP
         rows = pl.ds(first * CAP, GROUP_ROWS)
-        if part == 0:
-            for copy in token_copies[:GROUP]:
-                copy.wait_recv()
+        count = GROUP if part == 0 else OWN - GROUP
+        for copy in token_copies[first : first + count]:
+            copy.wait_recv()
         inputs = from_wire(token_recv[first : first + GROUP])
-        x_out[rows, :] = inputs
+        x_keep[rows, :] = inputs
         if part == 0:
             loads["gate"].wait()
             loads["up"].wait()
@@ -188,20 +189,26 @@
         sigmoid = 1.0 / (1.0 + jnp.exp(-gate))
         silu = gate * sigmoid
         active = silu * up
-        active_out[rows, :] = active.astype(jnp.bfloat16)
-        if part == 0:
-            for copy in weighted_copies[:GROUP]:
-                copy.wait_recv()
+        active_keep[rows, :] = active.astype(jnp.bfloat16)
+        return inputs, gate, up, sigmoid, silu, active
+
+    def front_out(part, kept):
+        inputs, gate, up, sigmoid, silu, active = kept
+        first = part * GROUP
+        rows = pl.ds(first * CAP, GROUP_ROWS)
+        count = GROUP if part == 0 else OWN - GROUP
+        for copy in weighted_copies[first : first + count]:
+            copy.wait_recv()
         upstream = from_wire(weighted_recv[first : first + GROUP])
-        weighted_out[rows, :] = upstream
+        weighted_keep[rows, :] = upstream
         if part == 0:
             loads["down"].wait()
         grad_active = dot(upstream, down_w[...], 1, 1)
         scalars = jnp.sum(grad_active * active, axis=1, keepdims=True)
         dgate = (grad_active * up * sigmoid * (1.0 + gate * (1.0 - sigmoid))).astype(jnp.bfloat16)
         dup = (grad_active * silu).astype(jnp.bfloat16)
-        dgate_out[rows, :] = dgate
-        dup_out[rows, :] = dup
+        dgate_keep[rows, :] = dgate
+        dup_keep[rows, :] = dup
         lane = lax.broadcasted_iota(jnp.int32, (8, 128), 1)
         for block in range(GROUP):
             eights = [jnp.broadcast_to(scalars[block * CAP + 8 * i : block * CAP + 8 * i + 8], (8, 128)) for i in range(3)]
@@ -217,70 +224,87 @@
             back_send[GROUP:OWN] = wire[: OWN - GROUP]
             back_out[OWN] = wire[OWN - GROUP]
 
-    front(0)
-    for copy in token_copies[GROUP:] + weighted_copies[GROUP:]:
-        copy.wait_recv()
-    for copy in back_copies[:GROUP] + dots_copies[:GROUP]:
-        copy.start()
-
-    for copy in y_sum:
-        copy.wait()
+    def gather(part, sems, device):
+        return remote(part, part, sems, device)
+
+    z_sum = remote(z_send.at[1 - my_zh], z_recv, (z_sems.at[0], z_sems.at[1]), z_twin)
+    near = whole_out.at[my_core, my_y, my_zh]
+    far = whole_out.at[my_core, my_y, 1 - my_zh]
+    z_gather = gather(near, (z_sems.at[2], z_sems.at[3]), z_twin)
+    y_near = [gather(near, (y_sems.at[2, step], y_sems.at[3, step]), y_twins[step]) for step in range(3)]
+    y_far = [gather(far, (y_sems.at[4, step], y_sems.at[5, step]), y_twins[step]) for step in range(3)]
+    core_near = gather(whole_out.at[my_core, :, my_zh], (core_sems.at[2], core_sems.at[3]), core_twin)
+    core_far = gather(whole_out.at[my_core, :, 1 - my_zh], (core_sems.at[4], core_sems.at[5]), core_twin)
+
+    def start(copies):
+        for copy in copies:
+            copy.start()
+
+    def wait(copies):
+        for copy in copies:
+            copy.wait()
+
+    kept = front_in(0)
+    wait(y_sum)
     mine = pl.ds(my_y * 2, 2)
-    y_total = drift_mine[mine] + f32(core_recv[mine])
-    for step in range(3):
-        y_total += f32(y_recv[step])
-    z_send[...] = y_total.astype(jnp.bfloat16)
-    z_sum = remote(z_send.at[1 - my_zh], z_recv, (z_sems.at[0], z_sems.at[1]), z_twin)
+    y_total[...] = drift_mine[mine] + f32(core_recv[mine]) + f32(y_recv[0]) + f32(y_recv[1]) + f32(y_recv[2])
+    z_send[...] = y_total[...].astype(jnp.bfloat16)
     z_sum.start()
-    near = jnp.where(my_zh == 0, y_total[0], y_total[1])
-    z_sum.wait()
-    average = (near + f32(z_recv[...])) / REPLICAS
-    average_out[...] = average
+    start(weighted_copies[GROUP + 2 :])
+    front_out(0, kept)
+    start(back_copies[:2] + dots_copies[:2])
+    kept = front_in(1)
     loads["outer"].wait()
     loads["momentum"].wait()
+    z_sum.wait()
+    average = (jnp.where(my_zh == 0, y_total[0], y_total[1]) + f32(z_recv[...])) / REPLICAS
+    average_out[...] = average
     moment = momentum_rate * momentum[...] + average
     stepped = outer[...] - outer_rate * (average + momentum_rate * moment)
-    whole_out[my_core, my_y, my_zh] = stepped.astype(jnp.bfloat16)
-    piece = whole_out.at[my_core, my_y, my_zh]
-    z_gather = remote(piece, piece, (z_sems.at[2], z_sems.at[3]), z_twin)
-    z_gather.start()
-
-    front(1)
-    for copy in back_copies[GROUP:] + dots_copies[GROUP:]:
-        copy.start()
-
+    near[...] = stepped.astype(jnp.bfloat16)
+    start([z_gather] + y_near)
+    start(back_copies[2:GROUP] + dots_copies[2:GROUP])
+    front_out(1, kept)
+    start(back_copies[GROUP:] + dots_copies[GROUP:])
     z_gather.wait()
-    y_gather = []
-    for step in range(3):
-        piece = whole_out.at[my_core, my_y]
-        copy = remote(piece, piece, (y_sems.at[2, step], y_sems.at[3, step]), y_twins[step])
-        copy.start()
-        y_gather.append(copy)
-    for copy in y_gather:
-        copy.wait()
-    piece = whole_out.at[my_core]
-    core_gather = remote(piece, piece, (core_sems.at[2], core_sems.at[3]), core_twin)
-    core_gather.start()
+    start(y_far)
+    wait(y_near)
+    core_near.start()
+
+    def wide_tile(index, carry):
+        columns = pl.ds(pl.multiple_of(index * 256, 256), 256)
+        inputs = x_keep[:, columns]
+        grad_gate_out[columns, :] = dot(inputs, dgate_keep[...], 0, 0).astype(jnp.bfloat16)
+        grad_up_out[columns, :] = dot(inputs, dup_keep[...], 0, 0).astype(jnp.bfloat16)
+        return carry
+
+    def down_tile(index, carry):
+        columns = pl.ds(pl.multiple_of(index * 128, 128), 128)
+        grad_down_out[columns, :] = dot(active_keep[:, columns], weighted_keep[...], 0, 0).astype(jnp.bfloat16)
+        return carry
+
+    lax.fori_loop(0, D // 256, wide_tile, 0)
+    wait(y_far)
+    core_far.start()
+    lax.fori_loop(0, FF // 128, down_tile, 0)
 
     for copy in token_copies + weighted_copies:
         copy.wait_send()
-    for copy in dots_copies:
-        copy.wait()
+    wait(dots_copies)
     for block in range(BLOCKS):
         for i in range(3):
-            start = block * CAP + 8 * i
-            dots_out[start : start + 8, :] = jnp.broadcast_to(dots_recv[block][:, 32 * i : 32 * i + 1], (8, 128))
-    for copy in back_copies:
-        copy.wait()
-    core_gather.wait()
+            first = block * CAP + 8 * i
+            dots_out[first : first + 8, :] = jnp.broadcast_to(dots_recv[block][:, 32 * i : 32 * i + 1], (8, 128))
+    wait(back_copies)
+    wait([core_near, core_far])
 
 
 def exchange(ids, logits, tokens, grads, w_gate, w_up, w_down, drift, outer, momentum):
     bf16, wide = jnp.bfloat16, jnp.float32
-    anywhere = pl.BlockSpec(memory_space=pl.ANY)
+    anywhere = pl.BlockSpec(memory_space=pltpu.HBM)
     inside = pl.BlockSpec(memory_space=pltpu.VMEM)
     outs = [
-        ((ROWS, D), bf16), ((ROWS, D), bf16), ((ROWS, FF), bf16), ((ROWS, FF), bf16), ((ROWS, FF), bf16),
+        ((D, FF), bf16), ((D, FF), bf16), ((FF, D), bf16),
         ((BLOCKS, 2 * CAP, HALF), bf16), ((ROWS, 128), bf16), ((ROWS, 128), wide),
         ((2, 128, 128), wide), ((2, 4, 2, 2, 128, 128), bf16),
     ]
@@ -293,6 +317,8 @@
         in_specs=[anywhere] * 10,
         out_specs=[inside] * len(outs),
         scratch_shapes=[
+            pltpu.VMEM((ROWS, D), bf16), pltpu.VMEM((ROWS, D), bf16), pltpu.VMEM((ROWS, FF), bf16),
+            pltpu.VMEM((ROWS, FF), bf16), pltpu.VMEM((ROWS, FF), bf16), pltpu.VMEM((2, 2, 128, 128), wide),
             pltpu.VMEM((1, 128), jnp.int32), pltpu.VMEM((8, 128), wide),
             pltpu.VMEM((128, D), bf16), pltpu.VMEM((128, D), bf16),
             pltpu.VMEM((D, FF), bf16), pltpu.VMEM((D, FF), bf16), pltpu.VMEM((FF, D), bf16),
@@ -302,81 +328,79 @@
             pltpu.VMEM((8, 2, 128, 128), bf16), pltpu.VMEM((8, 2, 128, 128), bf16),
             pltpu.VMEM((8, 2, 128, 128), bf16), pltpu.VMEM((3, 2, 2, 128, 128), bf16),
             pltpu.VMEM((2, 2, 128, 128), bf16), pltpu.VMEM((2, 128, 128), bf16),
-            dma((13,)), dma((4, OWN)), dma((4, OWN)), dma((4,)), dma((4, 3)), dma((4,)),
+            dma((13,)), dma((4, OWN)), dma((4, OWN)), dma((6,)), dma((6, 3)), dma((4,)),
         ],
         compiler_params=pltpu.CompilerParams(
-            collective_id=0, has_side_effects=True, vmem_limit_bytes=44 << 20
+            collective_id=0, has_side_effects=True, vmem_limit_bytes=32 << 20
         ),
         cost_estimate=pl.CostEstimate(flops=5 * 2 * ROWS * D * FF, bytes_accessed=16 << 20, transcendentals=ROWS * FF),
-    )(ids, logits, tokens, grads, w_gate, w_up, w_down, drift, outer, momentum)
-
-
-STEPS = 4
+    )(*[pltpu.with_memory_space_constraint(a, pltpu.HBM) for a in (ids, logits, tokens, grads, w_gate, w_up, w_down, drift, outer, momentum)])
 
 
 def finish_kernel(
-    x, weighted, active, dgate, dup, back, select, dots, average, whole, logits, outer, momentum, inner,
+    gate_in, up_in, down_in, back, select, dots, average, whole, logits, outer, momentum, inner,
     grad_tokens, grad_logits, grad_gate, grad_up, grad_down, new_outer, new_momentum, merged,
+    tokens_keep, logits_keep, outer_keep, momentum_keep, merged_keep, sems,
 ):
-    step = pl.program_id(0)
-    grad_gate[...] = dot(x[...], dgate[...], 0, 0).astype(jnp.bfloat16)
-    grad_up[...] = dot(x[...], dup[...], 0, 0).astype(jnp.bfloat16)
-    grad_down[...] = dot(active[...], weighted[...], 0, 0).astype(jnp.bfloat16)
-    for layer in range(2):
+    copies = []
+
+    def put(source, target):
+        copies.append(pltpu.make_async_copy(source, target, sems.at[len(copies)]))
+        copies[-1].start()
+
+    for source, target in ((gate_in, grad_gate), (up_in, grad_up), (down_in, grad_down)):
+        size = source.shape[0] // 4
+        for part in range(4):
+            put(source.at[pl.ds(part * size, size)], target.at[pl.ds(part * size, size)])
+    grad_tokens_rows = dot(select[...], from_wire(back[...]), 0, 0).astype(jnp.bfloat16)
+    tokens_keep[...] = grad_tokens_rows
+    put(tokens_keep, grad_tokens)
+    moment = momentum_rate * momentum[...] + average[...]
+    momentum_keep[...] = moment
+    put(momentum_keep, new_momentum)
+    outer_keep[...] = outer[...] - outer_rate * (average[...] + momentum_rate * moment)
+    put(outer_keep, new_outer)
+    scores = logits[...]
+    powers = jnp.exp(scores - jnp.max(scores, axis=0, keepdims=True))
+    probability = powers / jnp.sum(powers, axis=0, keepdims=True)
+    scalar = jnp.sum(f32(select[...]) * dots[...], axis=0, keepdims=True)
+    first = lax.broadcasted_iota(jnp.int32, (8, 128), 0) == 0
+    logits_keep[...] = jnp.where(first, scalar * (1.0 - probability), -probability * scalar)
+    put(logits_keep, grad_logits)
+    for y in range(4):
         for zh in range(2):
             for core in range(2):
-                rows = pl.ds((zh * 2 + core) * 128, 128)
-                merged[layer, rows, :] = (
-                    mix_rate * f32(inner[layer, rows, :]) + (1.0 - mix_rate) * f32(whole[core, 0, zh, layer])
-                ).astype(jnp.bfloat16)
-
-    @pl.when(step == 0)
-    def _():
-        grad_tokens[...] = dot(select[...], from_wire(back[...]), 0, 0).astype(jnp.bfloat16)
-        scores = logits[...]
-        powers = jnp.exp(scores - jnp.max(scores, axis=0, keepdims=True))
-        probability = powers / jnp.sum(powers, axis=0, keepdims=True)
-        scalar = jnp.sum(f32(select[...]) * dots[...], axis=0, keepdims=True)
-        first = lax.broadcasted_iota(jnp.int32, (8, 128), 0) == 0
-        grad_logits[...] = jnp.where(first, scalar * (1.0 - probability), -probability * scalar)
-        moment = momentum_rate * momentum[...] + average[...]
-        new_momentum[...] = moment
-        new_outer[...] = outer[...] - outer_rate * (average[...] + momentum_rate * moment)
-
-
-def finish(x, weighted, active, dgate, dup, back, select, dots, average, whole, logits, outer, momentum, inner):
+                rows = pl.ds(((y * 2 + zh) * 2 + core) * 128, 128)
+                for layer in range(2):
+                    merged_keep[layer, rows, :] = (
+                        mix_rate * f32(inner[layer, rows, :]) + (1.0 - mix_rate) * f32(whole[core, y, zh, layer])
+                    ).astype(jnp.bfloat16)
+    put(merged_keep, merged)
+    for copy in copies:
+        copy.wait()
+
+
+def finish(gate_in, up_in, down_in, back, select, dots, average, whole, logits, outer, momentum, inner):
     bf16, wide = jnp.bfloat16, jnp.float32
-
-    def fixed(shape):
-        return pl.BlockSpec(shape, lambda i: (0,) * len(shape))
-
-    x_cols, rows = D // STEPS, D // STEPS
+    anywhere = pl.BlockSpec(memory_space=pl.ANY)
+    inside = pl.BlockSpec(memory_space=pltpu.VMEM)
     return pl.pallas_call(
         finish_kernel,
-        grid=(STEPS,),
         out_shape=[
             jax.ShapeDtypeStruct((128, D), bf16), jax.ShapeDtypeStruct((8, 128), wide),
             jax.ShapeDtypeStruct((D, FF), bf16), jax.ShapeDtypeStruct((D, FF), bf16),
             jax.ShapeDtypeStruct((FF, D), bf16), jax.ShapeDtypeStruct((2, 128, 128), wide),
             jax.ShapeDtypeStruct((2, 128, 128), wide), jax.ShapeDtypeStruct((2, D, 128), bf16),
         ],
-        in_specs=[
-            pl.BlockSpec((ROWS, x_cols), lambda i: (0, i)), pl.BlockSpec((ROWS, x_cols), lambda i: (0, i)),
-            fixed((ROWS, FF)), fixed((ROWS, FF)), fixed((ROWS, FF)),
-            fixed((BLOCKS, 2 * CAP, HALF)), fixed((ROWS, 128)), fixed((ROWS, 128)), fixed((2, 128, 128)),
-            pl.BlockSpec((2, 1, 2, 2, 128, 128), lambda i: (0, i, 0, 0, 0, 0)),
-            fixed((8, 128)), fixed((2, 128, 128)), fixed((2, 128, 128)),
-            pl.BlockSpec((2, rows, 128), lambda i: (0, i, 0)),
+        in_specs=[anywhere] * 3 + [inside] * 9,
+        out_specs=[anywhere] * 8,
+        scratch_shapes=[
+            pltpu.VMEM((128, D), bf16), pltpu.VMEM((8, 128), wide), pltpu.VMEM((2, 128, 128), wide),
+            pltpu.VMEM((2, 128, 128), wide), pltpu.VMEM((2, D, 128), bf16), pltpu.SemaphoreType.DMA((17,)),
         ],
-        out_specs=[
-            fixed((128, D)), fixed((8, 128)),
-            pl.BlockSpec((x_cols, FF), lambda i: (i, 0)), pl.BlockSpec((x_cols, FF), lambda i: (i, 0)),
-            pl.BlockSpec((FF, x_cols), lambda i: (0, i)), fixed((2, 128, 128)), fixed((2, 128, 128)),
-            pl.BlockSpec((2, rows, 128), lambda i: (0, i, 0)),
-        ],
-        compiler_params=pltpu.CompilerParams(vmem_limit_bytes=44 << 20),
-        cost_estimate=pl.CostEstimate(flops=3 * 2 * ROWS * D * FF, bytes_accessed=18 << 20, transcendentals=1024),
-    )(x, weighted, active, dgate, dup, back, select, dots, average, whole, logits, outer, momentum, inner)
+        compiler_params=pltpu.CompilerParams(vmem_limit_bytes=20 << 20),
+        cost_estimate=pl.CostEstimate(flops=2 * ROWS * D * 128, bytes_accessed=22 << 20, transcendentals=1024),
+    )(gate_in, up_in, down_in, back, select, dots, average, whole, logits, outer, momentum, inner)
 
 
 def body(tokens, route_ids, route_logits, grad_out, w_gate, w_up, w_down, drift, outer, momentum, inner_now):

time: 62.8 us -> 49.7 us (0.79)
  local copies, waits for them, and re-layouts: 6.83 us -> 0.02 us
  Pallas kernels: 55 us -> 48.9 us
    unnamed x20 -> x8, local copies, waits for them, and re-layouts: 6.83 us -> 0.02 us
    pallas_call x1, Pallas kernels: 48.7 us -> 44.6 us  [exchange(): pl.pallas_call(exchange_kernel, out_shape=[jax.ShapeDtypeStruct(*out) for...]
    pallas_call x1, Pallas kernels: 6.34 us -> 4.34 us  [finish(): pl.pallas_call(finish_kernel, out_shape=[jax.ShapeDtypeStruct((128, D), b...]
where the time goes in v2:
time: 49.7 us; the launch traced here: 49.6 us
  Pallas kernels  48.9 us (98%)
  between operations  0.71 us (1%)
    pallas_call x1, Pallas kernels, exchange(): pl.pallas_call(exchange_kernel, out_shape=[jax.ShapeDtypeStruct(*out) for...  44.6 us
    pallas_call x1, Pallas kernels, finish(): pl.pallas_call(finish_kernel, out_shape=[jax.ShapeDtypeStruct((128, D), b...  4.34 us

profile of v2, /device:TPU:1, one launch (start us, length us, event | category | flops | bytes accessed | tf_op | source)
XLA Modules:
  0.0 49.6 jit_solution(6521278153459215626)
XLA Ops:
  0.6 0.0 copy-start
  0.6 0.0 copy-start.1
  0.7 0.0 copy-start.2
  0.7 0.0 copy-start.3
  0.7 44.6 %shard_map.170 = (bf16[2048,768]{1,0:T(8,128)(2,1)S(1)}, bf16[2048,768]{1,0:T(8,128)(2,1)S(1)}, bf16[768,2048]{1,0:T(8,128)(2,1)S(1)}, bf16[8,48,1024]{2,1,0:T(8...) custom-call(s32[1,128]{1,0:T(1,128)} %bitcast.19, ...), custom_call_target="tpu_custom_call" | custom-call | flops 3019898880 | bytes 16777216 | tf_op jit(solution)/shard_map/pallas_call | solution.py:314
  45.2 0.0 copy-done
  45.3 0.0 copy-done.1
  45.3 0.0 copy-done.2
  45.3 0.0 copy-done.3
  45.3 4.3 %shard_map.171 = (bf16[128,2048]{1,0:T(8,128)(2,1)}, f32[8,128]{1,0:T(8,128)}, bf16[2048,768]{1,0:T(8,128)(2,1)}, bf16[2048,768]{1,0:T(8,128)(2,1)}, bf16[768,20...) custom-call(bf16[2048,768]{1,0:T(8,128)(2,1)S(1)} %get-tuple-element.24.gate_in, ...), custom_call_target="tpu_custom_call" | custom-call | flops 100663296 | bytes 23068672 | tf_op jit(solution)/shard_map/pallas_call | solution.py:387
Async XLA Ops:
  0.6 44.6 %copy-start = (bf16[1,2,2048,128]{3,2,1,0:T(8,128)(2,1)S(1)}, bf16[1,2,2048,128]{3,2,1,0:T(8,128)(2,1)}, u32[]{:S(2)}) copy-start(bf16[1,2,2048,128]{3,2,1,0:T(8,128)(2,1)} %param.21) | copy-start | bytes 3145732
  0.6 44.6 %copy-start.1 = (f32[2,128,128]{2,1,0:T(8,128)S(1)}, f32[2,128,128]{2,1,0:T(8,128)}, u32[]{:S(2)}) copy-start(f32[2,128,128]{2,1,0:T(8,128)} %outer.1) | copy-start | bytes 393220
  0.7 44.6 %copy-start.2 = (f32[2,128,128]{2,1,0:T(8,128)S(1)}, f32[2,128,128]{2,1,0:T(8,128)}, u32[]{:S(2)}) copy-start(f32[2,128,128]{2,1,0:T(8,128)} %momentum.1) | copy-start | bytes 393220
  0.7 44.6 %copy-start.3 = (f32[128,8]{0,1:T(8,128)S(1)}, f32[128,8]{0,1:T(8,128)}, u32[]{:S(2)}) copy-start(f32[128,8]{0,1:T(8,128)} %param.13) | copy-start | bytes 12292

commit v3 on v2

--- a/solution.py
+++ b/solution.py
@@ -20,7 +20,7 @@
 outer_rate = 0.7
 mix_rate = 0.5
 
-OFFSETS = ((1, 0), (3, 0), (1, 1), (3, 1), (2, 0), (2, 1), (0, 1), (0, 0))
+OFFSETS = ((1, 0), (3, 0), (1, 1), (3, 1), (2, 1), (2, 0), (0, 1), (0, 0))
 OWN = 7
 
 
@@ -134,8 +134,8 @@
     values = tokens[...]
     place(0, values, token_send, token_recv)
     pl.semaphore_wait(barrier, len(partners))
-    for copy in token_copies[:GROUP]:
-        copy.start()
+    for block in (2, 3, 0, 1):
+        token_copies[block].start()
 
     core_sum = remote(core_send, core_recv, (core_sems.at[0], core_sems.at[1]), core_twin)
     loads["other0"].wait()
@@ -151,8 +151,8 @@
     loads["grads"].wait()
     weighted = (f32(grads[...]) * jnp.concatenate([column] * (D // 128), axis=1)).astype(jnp.bfloat16)
     place(0, weighted, weighted_send, weighted_recv)
-    for copy in weighted_copies[:GROUP]:
-        copy.start()
+    for block in (2, 3, 0, 1):
+        weighted_copies[block].start()
     place(1, values, token_send, token_recv)
     for copy in token_copies[GROUP:]:
         copy.start()
@@ -252,7 +252,7 @@
     z_sum.start()
     start(weighted_copies[GROUP + 2 :])
     front_out(0, kept)
-    start(back_copies[:2] + dots_copies[:2])
+    start(dots_copies[:GROUP] + back_copies[:2])
     kept = front_in(1)
     loads["outer"].wait()
     loads["momentum"].wait()
@@ -263,9 +263,9 @@
     stepped = outer[...] - outer_rate * (average + momentum_rate * moment)
     near[...] = stepped.astype(jnp.bfloat16)
     start([z_gather] + y_near)
-    start(back_copies[2:GROUP] + dots_copies[2:GROUP])
+    start(back_copies[2:GROUP])
     front_out(1, kept)
-    start(back_copies[GROUP:] + dots_copies[GROUP:])
+    start(dots_copies[GROUP:] + back_copies[GROUP:])
     z_gather.wait()
     start(y_far)
     wait(y_near)

time: 49.7 us -> 48.1 us (0.968)
  Pallas kernels: 48.9 us -> 47.2 us
    pallas_call x1, Pallas kernels: 44.6 us -> 42.9 us  [exchange(): pl.pallas_call(exchange_kernel, out_shape=[jax.ShapeDtypeStruct(*out) for...]
where the time goes in v3:
time: 48.1 us; the launch traced here: 47.9 us
  Pallas kernels  47.2 us (98%)
  between operations  0.71 us (1%)
    pallas_call x1, Pallas kernels, exchange(): pl.pallas_call(exchange_kernel, out_shape=[jax.ShapeDtypeStruct(*out) for...  42.9 us
    pallas_call x1, Pallas kernels, finish(): pl.pallas_call(finish_kernel, out_shape=[jax.ShapeDtypeStruct((128, D), b...  4.34 us

profile of v3, /device:TPU:1, one launch (start us, length us, event | category | flops | bytes accessed | tf_op | source)
XLA Modules:
  0.0 47.9 jit_solution(14044009420070281952)
XLA Ops:
  0.6 0.0 copy-start
  0.6 0.0 copy-start.1
  0.7 0.0 copy-start.2
  0.7 0.0 copy-start.3
  0.7 42.9 %shard_map.170 = (bf16[2048,768]{1,0:T(8,128)(2,1)S(1)}, bf16[2048,768]{1,0:T(8,128)(2,1)S(1)}, bf16[768,2048]{1,0:T(8,128)(2,1)S(1)}, bf16[8,48,1024]{2,1,0:T(8...) custom-call(s32[1,128]{1,0:T(1,128)} %bitcast.19, ...), custom_call_target="tpu_custom_call" | custom-call | flops 3019898880 | bytes 16777216 | tf_op jit(solution)/shard_map/pallas_call | solution.py:314
  43.6 0.0 copy-done
  43.6 0.0 copy-done.1
  43.6 0.0 copy-done.2
  43.6 0.0 copy-done.3
  43.6 4.3 %shard_map.171 = (bf16[128,2048]{1,0:T(8,128)(2,1)}, f32[8,128]{1,0:T(8,128)}, bf16[2048,768]{1,0:T(8,128)(2,1)}, bf16[2048,768]{1,0:T(8,128)(2,1)}, bf16[768,20...) custom-call(bf16[2048,768]{1,0:T(8,128)(2,1)S(1)} %get-tuple-element.24.gate_in, ...), custom_call_target="tpu_custom_call" | custom-call | flops 100663296 | bytes 23068672 | tf_op jit(solution)/shard_map/pallas_call | solution.py:387
Async XLA Ops:
  0.6 42.9 %copy-start = (bf16[1,2,2048,128]{3,2,1,0:T(8,128)(2,1)S(1)}, bf16[1,2,2048,128]{3,2,1,0:T(8,128)(2,1)}, u32[]{:S(2)}) copy-start(bf16[1,2,2048,128]{3,2,1,0:T(8,128)(2,1)} %param.21) | copy-start | bytes 3145732
  0.6 42.9 %copy-start.1 = (f32[2,128,128]{2,1,0:T(8,128)S(1)}, f32[2,128,128]{2,1,0:T(8,128)}, u32[]{:S(2)}) copy-start(f32[2,128,128]{2,1,0:T(8,128)} %outer.1) | copy-start | bytes 393220
  0.7 42.9 %copy-start.2 = (f32[2,128,128]{2,1,0:T(8,128)S(1)}, f32[2,128,128]{2,1,0:T(8,128)}, u32[]{:S(2)}) copy-start(f32[2,128,128]{2,1,0:T(8,128)} %momentum.1) | copy-start | bytes 393220
  0.7 42.9 %copy-start.3 = (f32[128,8]{0,1:T(8,128)S(1)}, f32[128,8]{0,1:T(8,128)}, u32[]{:S(2)}) copy-start(f32[128,8]{0,1:T(8,128)} %param.13) | copy-start | bytes 12292

commit v4 on v3

--- a/solution.py
+++ b/solution.py
@@ -165,7 +165,7 @@
     core_sum.wait()
     y_send[...] = (drift_mine[...] + f32(core_recv[...])).astype(jnp.bfloat16)
     y_sum = []
-    for step in range(3):
+    for step in (1, 0, 2):
         there = (my_y + step + 1) % 4
         copy = remote(
             y_send.at[pl.ds(there * 2, 2)], y_recv.at[step], (y_sems.at[0, step], y_sems.at[1, step]), y_twins[step]
@@ -231,8 +231,8 @@
     near = whole_out.at[my_core, my_y, my_zh]
     far = whole_out.at[my_core, my_y, 1 - my_zh]
     z_gather = gather(near, (z_sems.at[2], z_sems.at[3]), z_twin)
-    y_near = [gather(near, (y_sems.at[2, step], y_sems.at[3, step]), y_twins[step]) for step in range(3)]
-    y_far = [gather(far, (y_sems.at[4, step], y_sems.at[5, step]), y_twins[step]) for step in range(3)]
+    y_near = [gather(near, (y_sems.at[2, step], y_sems.at[3, step]), y_twins[step]) for step in (1, 0, 2)]
+    y_far = [gather(far, (y_sems.at[4, step], y_sems.at[5, step]), y_twins[step]) for step in (1, 0, 2)]
     core_near = gather(whole_out.at[my_core, :, my_zh], (core_sems.at[2], core_sems.at[3]), core_twin)
     core_far = gather(whole_out.at[my_core, :, 1 - my_zh], (core_sems.at[4], core_sems.at[5]), core_twin)
 

time: 48.1 us -> 48.3 us (level)
  no operation moved by 1% of the time
where the time goes in v4:
time: 48.3 us; the launch traced here: 48.2 us
  Pallas kernels  47.5 us (98%)
  between operations  0.71 us (1%)
    pallas_call x1, Pallas kernels, exchange(): pl.pallas_call(exchange_kernel, out_shape=[jax.ShapeDtypeStruct(*out) for...  43.2 us
    pallas_call x1, Pallas kernels, finish(): pl.pallas_call(finish_kernel, out_shape=[jax.ShapeDtypeStruct((128, D), b...  4.34 us

profile of v4, /device:TPU:1, one launch (start us, length us, event | category | flops | bytes accessed | tf_op | source)
XLA Modules:
  0.0 48.2 jit_solution(7708153681659530360)
XLA Ops:
  0.6 0.0 copy-start
  0.6 0.0 copy-start.1
  0.7 0.0 copy-start.2
  0.7 0.0 copy-start.3
  0.7 43.2 %shard_map.170 = (bf16[2048,768]{1,0:T(8,128)(2,1)S(1)}, bf16[2048,768]{1,0:T(8,128)(2,1)S(1)}, bf16[768,2048]{1,0:T(8,128)(2,1)S(1)}, bf16[8,48,1024]{2,1,0:T(8...) custom-call(s32[1,128]{1,0:T(1,128)} %bitcast.19, ...), custom_call_target="tpu_custom_call" | custom-call | flops 3019898880 | bytes 16777216 | tf_op jit(solution)/shard_map/pallas_call | solution.py:314
  43.8 0.0 copy-done
  43.8 0.0 copy-done.1
  43.9 0.0 copy-done.2
  43.9 0.0 copy-done.3
  43.9 4.3 %shard_map.171 = (bf16[128,2048]{1,0:T(8,128)(2,1)}, f32[8,128]{1,0:T(8,128)}, bf16[2048,768]{1,0:T(8,128)(2,1)}, bf16[2048,768]{1,0:T(8,128)(2,1)}, bf16[768,20...) custom-call(bf16[2048,768]{1,0:T(8,128)(2,1)S(1)} %get-tuple-element.24.gate_in, ...), custom_call_target="tpu_custom_call" | custom-call | flops 100663296 | bytes 23068672 | tf_op jit(solution)/shard_map/pallas_call | solution.py:387
Async XLA Ops:
  0.6 43.2 %copy-start = (bf16[1,2,2048,128]{3,2,1,0:T(8,128)(2,1)S(1)}, bf16[1,2,2048,128]{3,2,1,0:T(8,128)(2,1)}, u32[]{:S(2)}) copy-start(bf16[1,2,2048,128]{3,2,1,0:T(8,128)(2,1)} %param.21) | copy-start | bytes 3145732
  0.6 43.2 %copy-start.1 = (f32[2,128,128]{2,1,0:T(8,128)S(1)}, f32[2,128,128]{2,1,0:T(8,128)}, u32[]{:S(2)}) copy-start(f32[2,128,128]{2,1,0:T(8,128)} %outer.1) | copy-start | bytes 393220
  0.7 43.2 %copy-start.2 = (f32[2,128,128]{2,1,0:T(8,128)S(1)}, f32[2,128,128]{2,1,0:T(8,128)}, u32[]{:S(2)}) copy-start(f32[2,128,128]{2,1,0:T(8,128)} %momentum.1) | copy-start | bytes 393220
  0.7 43.2 %copy-start.3 = (f32[128,8]{0,1:T(8,128)S(1)}, f32[128,8]{0,1:T(8,128)}, u32[]{:S(2)}) copy-start(f32[128,8]{0,1:T(8,128)} %param.13) | copy-start | bytes 12292
